TPU v7x, 256 devices: a whole 4x4x8 slice. The times are simulated.
256 devices in a mesh: dp: 16 (over z, core), seq: 16 (over y, x).
Axes of the slice: x: 4, y: 4, z: 8, core: 2. Of those that a mesh axis runs over, the one named last changes fastest.
Arguments:
- tokens: bfloat16 [16, 16, 320, 1152], P('dp', 'seq'), may hold values from -6 to 6
- cotangent: bfloat16 [16, 16, 320, 1152], P('dp', 'seq'), may hold values from -6 to 6
- modulation: float32 [16, 6, 1152], P('dp'), may hold values from -3 to 3
- lengths: int32 [16], P('dp'), may hold values from 1 to 16, as said below
- w_spatial_qkv: bfloat16 [1152, 1728], replicated, may hold values from -1 to 1
- w_spatial_out: bfloat16 [576, 1152], replicated, may hold values from -0.25 to 0.25
- w_temporal_qkv: bfloat16 [1152, 1728], replicated, may hold values from -1 to 1
- w_temporal_out: bfloat16 [576, 1152], replicated, may hold values from -0.25 to 0.25
Outputs:
- grad_tokens: bfloat16 [16, 16, 320, 1152], P('dp', 'seq')
- grad_spatial_qkv: bfloat16 [1152, 1728], P('seq')
- grad_spatial_out: bfloat16 [576, 1152], P('seq')
- grad_temporal_qkv: bfloat16 [1152, 1728], P('seq')
- grad_temporal_out: bfloat16 [576, 1152], P('seq')
Inputs may be any that keep to these rules, and one draw needn't show every extreme that they name: `lengths`: frames of each clip that hold data; later frames are padding. Some clip holds all 16 frames and some other clip only its first.
All inputs are finite; a program needn't handle non-finite values.
Results may differ from a plain program's by a relative error of at most 0.04.
Values may be sent and summed in bfloat16 or wider, within the bound.
A program may use at most 192 MiB of HBM per device.

v0:
```python
import jax
import jax.numpy as jnp
from jax import lax
from jax.experimental import pallas as pl
from jax.experimental.pallas import tpu as pltpu
from jax.sharding import PartitionSpec as P

HEADS = 8
HEAD_DIM = 72
F = 16
SIDE = 4
NZ = 8
BLOCKS = 16
WIDE = 2304
HALF = 1152
VMEM_LIMIT = 63 * 1024 * 1024


def remote(src, dst, send, recv, device):
    return pltpu.make_async_remote_copy(
        src_ref=src,
        dst_ref=dst,
        send_sem=send,
        recv_sem=recv,
        device_id=device,
        device_id_type=pl.DeviceIdType.MESH,
    )


def hail(devices):
    barrier = pltpu.get_barrier_semaphore()
    for device in devices:
        pl.semaphore_signal(barrier, inc=1, device_id=device, device_id_type=pl.DeviceIdType.MESH)


def meet(devices):
    pl.semaphore_wait(pltpu.get_barrier_semaphore(), len(devices))


class Exchange:
    def __init__(self, place, source, into, own_sem, send_sems, recv_sems):
        self.place, self.source, self.into = place, source, into
        self.own_sem, self.send_sems, self.recv_sems = own_sem, send_sems, recv_sems

    def to(self, d):
        return lax.rem(self.place.seq + d, BLOCKS)

    def copy(self, d):
        at = self.place
        return remote(
            self.source.at[self.to(d)],
            self.into.at[at.seq],
            self.send_sems.at[d],
            self.recv_sems.at[d],
            (at.dp, self.to(d)),
        )

    def own(self):
        me = self.place.seq
        return pltpu.make_async_copy(self.source.at[me], self.into.at[me], self.own_sem)

    def start(self):
        self.own().start()
        for d in range(1, BLOCKS):
            self.copy(d).start()

    def arrive(self):
        at = self.place
        for d in range(1, BLOCKS):
            origin = lax.rem(at.seq + BLOCKS - d, BLOCKS)
            remote(
                self.source.at[origin],
                self.into.at[origin],
                self.send_sems.at[d],
                self.recv_sems.at[d],
                (at.dp, origin),
            ).wait_recv()
        self.own().wait()

    def settle(self):
        for d in range(1, BLOCKS):
            self.copy(d).wait_send()


def exchange_sems():
    dma = pltpu.SemaphoreType.DMA
    return [dma, dma((BLOCKS,)), dma((BLOCKS,))]


def plus(*refs):
    total = refs[0].astype(jnp.float32)
    for ref in refs[1:]:
        total = total + ref.astype(jnp.float32)
    return total.astype(jnp.bfloat16)


CUTS = ((0, 640), (640, 512))
DMA_COUNTS = (
    (BLOCKS, 2),
    (2, 2, 2),
    (2, 2, SIDE),
    (2, SIDE),
)


class Place:
    def __init__(self):
        dp, seq = lax.axis_index("dp"), lax.axis_index("seq")
        self.dp, self.seq = dp, seq
        self.z, self.c = lax.div(dp, 2), lax.rem(dp, 2)
        self.y, self.x = lax.div(seq, SIDE), lax.rem(seq, SIDE)
        self.twin = (self.z * 2 + 1 - self.c, seq)

    def neighbour(self, axis, dirn):
        step = 1 if dirn == 0 else SIDE - 1
        if axis == 0:
            return (self.dp, self.y * SIDE + lax.rem(self.x + step, SIDE))
        return (self.dp, lax.rem(self.y + step, SIDE) * SIDE + self.x)

    def along_z(self, d):
        return (lax.rem(self.z + d, NZ) * 2 + self.c, self.seq)

    def line(self):
        return [(self.dp, lax.rem(self.seq + d, BLOCKS)) for d in range(1, BLOCKS)]

    def friends(self):
        return [self.twin] + self.line() + [self.along_z(d) for d in range(1, NZ)]


class Reduction:
    def __init__(self, place, grads, buffers, sems):
        self.place, self.grads = place, grads
        self.acc, self.near, self.far, self.last = buffers
        (
            self.core_send,
            self.core_recv,
            self.near_send,
            self.near_recv,
            self.far_send,
            self.far_recv,
            self.last_send,
            self.last_recv,
        ) = sems

    def lanes(self, part):
        return pl.ds(CUTS[part][0], CUTS[part][1])

    def lanes_of(self, part, core):
        return pl.ds(pl.multiple_of(core * HALF + CUTS[part][0], 128), CUTS[part][1])

    def block(self, part, j, d):
        at = self.place
        if part == 0:
            return j * SIDE + lax.rem(at.x + d, SIDE)
        return lax.rem(at.y + d, SIDE) * SIDE + j

    def core_copy(self, part, b):
        at = self.place
        return remote(
            self.grads.at[b, :, self.lanes_of(part, 1 - at.c)],
            self.acc.at[b, :, self.lanes(part)],
            self.core_send.at[b, part],
            self.core_recv.at[b, part],
            at.twin,
        )

    def near_copy(self, part, dirn, k, b):
        return remote(
            self.acc.at[b, :, self.lanes(part)],
            self.near.at[part, dirn, k, :, pl.ds(0, CUTS[part][1])],
            self.near_send.at[part, dirn, k],
            self.near_recv.at[part, dirn, k],
            self.place.neighbour(part, dirn),
        )

    def far_copy(self, part, dirn, j, b):
        return remote(
            self.acc.at[b, :, self.lanes(part)],
            self.far.at[part, dirn, j, :, pl.ds(0, CUTS[part][1])],
            self.far_send.at[part, dirn, j],
            self.far_recv.at[part, dirn, j],
            self.place.neighbour(part, dirn),
        )

    def last_copy(self, part, d, b):
        at = self.place
        if part == 0:
            to = (at.dp, lax.rem(at.y + d, SIDE) * SIDE + at.x)
        else:
            to = (at.dp, at.y * SIDE + lax.rem(at.x + d, SIDE))
        return remote(
            self.acc.at[b, :, self.lanes(part)],
            self.last.at[part, d, :, pl.ds(0, CUTS[part][1])],
            self.last_send.at[part, d],
            self.last_recv.at[part, d],
            to,
        )

    def gather(self, part, b, *more):
        self.core_copy(part, b).wait_recv()
        lanes = self.lanes(part)
        mine = self.grads[b, :, self.lanes_of(part, self.place.c)]
        self.acc[b, :, lanes] = plus(mine, self.acc[b, :, lanes], *more)

    def start(self):
        for d in (2, 1, 3, 0):

            @pl.loop(0, SIDE)
            def _(j):
                for part in range(2):
                    self.core_copy(part, self.block(part, j, d)).start()

    def first(self):
        for dirn in range(2):

            @pl.loop(0, 2)
            def _(k):
                for part in range(2):
                    b = self.block(part, 2 * dirn + k, 2)
                    self.gather(part, b)
                    self.near_copy(part, dirn, k, b).start()

    def second(self):
        for dirn in range(2):

            @pl.loop(0, 2)
            def _(k):
                for part in range(2):
                    j = 2 * (1 - dirn) + k
                    b = self.block(part, j, 1 + 2 * dirn)
                    self.gather(part, b)
                    self.far_copy(part, dirn, j, b).start()

    def third(self):
        for dirn in range(2):

            @pl.loop(0, 2)
            def _(k):
                for part in range(2):
                    j = 2 * dirn + k
                    b = self.block(part, j, 1 + 2 * dirn)
                    self.near_copy(part, dirn, k, b).wait_recv()
                    self.gather(part, b, self.near[part, dirn, k, :, pl.ds(0, CUTS[part][1])])
                    self.far_copy(part, dirn, j, b).start()

    def finish(self, part, d):
        at = self.place
        b = self.block(1 - part, (at.x, at.y)[part], d)
        j = lax.rem((at.y, at.x)[part] + d, SIDE)
        for dirn in range(2):
            self.far_copy(part, dirn, j, b).wait_recv()
        width = pl.ds(0, CUTS[part][1])
        self.gather(part, b, self.far[part, 0, j, :, width], self.far[part, 1, j, :, width])
        return b

    def fourth(self):
        for d in (2, 1, 3):
            for part in range(2):
                self.last_copy(part, d, self.finish(part, d)).start()

    def fifth(self, final):
        for part in range(2):
            b = self.finish(part, 0)
            total = wide(self.acc[b, :, self.lanes(part)])
            start, width = CUTS[part]
            for d in range(1, SIDE):
                self.last_copy(part, d, b).wait_recv()
                total = total + wide(self.last[part, d, :, pl.ds(0, width)])
            for n in range(0, width, 128):
                final[(start + n) // 128] = total[:, n : n + 128].astype(jnp.bfloat16)

    def settle(self):
        for part in range(2):

            @pl.loop(0, BLOCKS)
            def _(b):
                self.core_copy(part, b).wait_send()

            for dirn in range(2):

                @pl.loop(0, 2)
                def _(k):
                    self.near_copy(part, dirn, k, 0).wait_send()

                @pl.loop(0, SIDE)
                def _(j):
                    self.far_copy(part, dirn, j, 0).wait_send()

            for d in range(1, SIDE):
                self.last_copy(part, d, 0).wait_send()


def reduction_buffers():
    half = jnp.bfloat16
    return [
        pltpu.VMEM((2, 2, 2, 72, 640), half),
        pltpu.VMEM((2, 2, SIDE, 72, 640), half),
        pltpu.VMEM((2, SIDE, 72, 640), half),
    ]


def reduction_sems():
    return [pltpu.SemaphoreType.DMA(counts) for counts in DMA_COUNTS for _ in range(2)]


class Depth:
    def __init__(self, place, final, out, arrived, sems):
        self.place, self.final, self.out = place, final, out
        self.arrived = arrived
        self.up_send, self.up_recv, self.down_send, self.down_recv, self.pair_send, self.pair_recv = sems

    def spot(self, i, core):
        return self.out.at[core, TILES[i][0]]

    def device(self, z):
        return (z * 2 + self.place.c, self.place.seq)

    def up(self, i, z):
        tile, owner, slot = TILES[i]
        return remote(
            self.final.at[tile],
            self.arrived.at[slot, z],
            self.up_send.at[i],
            self.up_recv.at[i, z],
            self.device(owner),
        )

    def down(self, i, z):
        spot = self.spot(i, self.place.c)
        return remote(spot, spot, self.down_send.at[i, z], self.down_recv.at[i], self.device(z))

    def pair(self, i, core):
        spot = self.spot(i, core)
        return remote(spot, spot, self.pair_send.at[i], self.pair_recv.at[i], self.place.twin)

    def owned(self, body):
        for i, (_, owner, _) in enumerate(TILES):
            pl.when(self.place.z == owner)(lambda i=i: body(i))

    def others(self, body):
        for i, (_, owner, _) in enumerate(TILES):
            pl.when(self.place.z != owner)(lambda i=i: body(i))

    def away(self, i):
        return [z for z in range(NZ) if z != TILES[i][1]]

    def start(self):
        self.others(lambda i: self.up(i, self.place.z).start())

    def middle(self):
        def add(i):
            tile, _, slot = TILES[i]
            total = self.final[tile].astype(jnp.float32)
            for z in self.away(i):
                self.up(i, z).wait_recv()
                total = total + self.arrived[slot, z].astype(jnp.float32)
            self.spot(i, self.place.c)[...] = total.astype(jnp.bfloat16)
            for z in self.away(i):
                self.down(i, z).start()
            self.pair(i, self.place.c).start()

        self.owned(add)

    def end(self):
        def forward(i):
            self.down(i, self.place.z).wait_recv()
            self.pair(i, self.place.c).start()

        self.others(forward)
        for i in range(len(TILES)):
            self.pair(i, 1 - self.place.c).wait_recv()

    def settle(self):
        self.others(lambda i: self.up(i, self.place.z).wait_send())

        def left(i):
            for z in self.away(i):
                self.down(i, z).wait_send()

        self.owned(left)
        for i in range(len(TILES)):
            self.pair(i, self.place.c).wait_send()


TILES = tuple((k, k % NZ, k // NZ) for k in range(9))


def depth_sems():
    dma = pltpu.SemaphoreType.DMA
    n = len(TILES)
    return [dma((n,)), dma((n, NZ)), dma((n, NZ)), dma((n,)), dma((n,)), dma((n,))]


NORM_EPS = 1e-06
MASKED = -1e30
ROWS = 320
SPAN = 8
GROUPS = 3
GROUP = SPAN * BLOCKS
SPREAD = GROUPS * GROUP
ODD = 4
D = 1152
INNER = 576
QKV = 1728
UNROLL = 2
NARROW = 640
REST = D - NARROW
SHARP = HEAD_DIM ** (-0.5)
SHARP2 = SHARP * 1.4426950408889634
NN = (((1,), (0,)), ((), ()))
NT = (((1,), (1,)), ((), ()))
TN = (((0,), (0,)), ((), ()))
HALF16 = jnp.bfloat16


def matmul(left, right, dims=NN):
    return lax.dot_general(left, right, dims, preferred_element_type=jnp.float32)


def columns(total, width=256):
    return [(start, min(width, total - start)) for start in range(0, total, width)]


def normalise(source):
    average = jnp.mean(source, axis=-1, keepdims=True)
    centred = source - average
    variance = jnp.mean(centred * centred, axis=-1, keepdims=True)
    spread = lax.rsqrt(variance + NORM_EPS)
    return centred * spread, spread


def modulated(source, mod, first):
    unit, _ = normalise(source)
    return (unit * (1.0 + mod[first + 1]) + mod[first]).astype(HALF16)


def norm_pullback(source, upstream, gain):
    unit, spread = normalise(source)
    grad = upstream * gain
    along = jnp.mean(grad * unit, axis=-1, keepdims=True)
    return spread * (grad - jnp.mean(grad, axis=-1, keepdims=True) - unit * along)


def wide(ref_value):
    return ref_value.astype(jnp.float32)


def by_columns(total, width, body):
    even = total // width * width

    @pl.loop(0, even, step=width)
    def _(start):
        body(pl.multiple_of(start, width), width)

    if even < total:
        body(even, total - even)


def project_rows(rows_ref, rows, weight_ref, out_ref, out_rows):
    def body(start, width):
        cols = pl.ds(start, width)
        out_ref[out_rows, cols] = matmul(rows_ref[rows, :], weight_ref[cols, :], NT).astype(HALF16)

    by_columns(weight_ref.shape[0], 512, body)


def spread_heads(wide_ref, heads_ref, count, rows):
    for i in range(count):
        heads_ref[i, rows] = wide_ref[rows, i * HEAD_DIM : (i + 1) * HEAD_DIM]


def softmax(scores, axis):
    exponent = jnp.exp2((scores - jnp.max(scores, axis=axis, keepdims=True)) * SHARP2)
    return exponent * (1.0 / jnp.sum(exponent, axis=axis, keepdims=True))


def attend_spatial(heads, mixed_heads, rows):
    def body(h, _):
        scores = matmul(heads[h, rows], heads[HEADS + h], NT)
        soft = softmax(scores, -1).astype(HALF16)
        mixed_heads[h, rows] = matmul(soft, heads[2 * HEADS + h]).astype(HALF16)
        return 0

    lax.fori_loop(0, HEADS, body, 0, unroll=UNROLL)


def head_back(queries, keys, values, upstream, bias=None):
    scores = matmul(keys, queries, NT)
    if bias is not None:
        scores = scores + bias
    soft = softmax(scores, 0)
    soft_rounded = soft.astype(HALF16)
    raw = matmul(values, upstream, NT)
    centred = raw - jnp.sum(raw * soft, axis=0, keepdims=True)
    grad_scores = (soft * centred).astype(HALF16)
    grad_values = matmul(soft_rounded, upstream).astype(HALF16)
    grad_keys = (matmul(grad_scores, queries) * SHARP).astype(HALF16)
    grad_queries = (matmul(grad_scores, keys, TN) * SHARP).astype(HALF16)
    return grad_queries, grad_keys, grad_values, soft_rounded


def qkv_blocks(depth, tall, packed_grads, grads):
    deep = slice(0, depth)

    def body(start, width):
        cols = pl.ds(start, width)
        product = matmul(tall[:, deep], packed_grads[deep, cols])
        grads[:, :, cols] = product.reshape(BLOCKS, 72, width).astype(HALF16)

    by_columns(QKV, 256, body)


def out_blocks(depth, inner_tall, cot, low, high, grads):
    deep = slice(0, depth)
    low[:, deep] = jnp.zeros((D, depth), jnp.float32)
    high[:, deep] = jnp.zeros((D, depth), jnp.float32)
    for s in range(BLOCKS):
        rows = inner_tall[s * 36 : (s + 1) * 36, deep]
        low[s * 72 : s * 72 + 36, deep] = rows
        high[s * 72 + 36 : (s + 1) * 72, deep] = rows
    low_rows, high_rows = low[:, deep].astype(HALF16), high[:, deep].astype(HALF16)
    for start, width in ((0, 192), (192, 192), (384, 192)):
        product = matmul(low_rows, cot[deep, start : start + width]) + matmul(
            high_rows, cot[deep, INNER + start : INNER + start + width]
        )
        grads[:, :, QKV + start : QKV + start + width] = product.reshape(BLOCKS, 72, width).astype(
            HALF16
        )


def transposed(rows_ref, count, tall_ref):
    for start, width in columns(D, 128):
        cols = slice(start, start + width)
        tall_ref[cols, 0:count] = rows_ref[0:count, cols].T


def upstream_of(packed_grads, rows, w_qkv, into, count):
    def body(start, width):
        into[pl.ds(start, count), :] = matmul(packed_grads[rows, :], w_qkv[:, pl.ds(start, width)])

    by_columns(D, SPREAD, body)


def upstream_rows(into, start, count):
    return jnp.concatenate(
        [into[n * SPREAD + start : n * SPREAD + start + count, :] for n in range(3)], axis=-1
    )


def fold_odd(flat, first, step, pad, blocks):
    for i in range(BLOCKS):
        rows = slice(first + i * step, first + i * step + ODD)
        pad[i * SPAN : i * SPAN + ODD, :] = flat[rows, 0:NARROW]
        pad[i * SPAN + ODD : (i + 1) * SPAN, 0:REST] = flat[rows, NARROW:D]
    blocks[...] = pad[...].reshape(BLOCKS, SPAN, NARROW).astype(HALF16)


def unfold_odd(blocks, pad, flat, first, step):
    pad[...] = wide(blocks[...]).reshape(GROUP, NARROW)
    for i in range(BLOCKS):
        rows = slice(first + i * step, first + i * step + ODD)
        flat[rows, 0:NARROW] = pad[i * SPAN : i * SPAN + ODD, :]
        flat[rows, NARROW:D] = pad[i * SPAN + ODD : (i + 1) * SPAN, 0:REST]


def assemble(tiles, summed, start):
    for k in range(18):
        summed[:, start + k * 128 : start + (k + 1) * 128] = tiles[k // 9, k % 9]


def as_blocks(rows):
    return rows.reshape(BLOCKS, SPAN, D).astype(HALF16)


def kernel(
    lengths,
    mod,
    tokens_far,
    cot_far,
    w_spatial_qkv_far,
    w_spatial_out_far,
    w_temporal_qkv_far,
    w_temporal_out_far,
    grad_tokens,
    summed,
    tokens,
    cot,
    w_spatial_qkv,
    w_spatial_out,
    w_temporal_qkv,
    w_temporal_out,
    load_sems,
    cot_blocks,
    cot_place,
    resid_blocks,
    resid_place,
    grad_place,
    cot_odd,
    cot_odd_place,
    resid_odd,
    resid_odd_place,
    grad_odd_place,
    pad,
    flat,
    packed,
    heads,
    mixed_heads,
    mixed,
    normed_time,
    packed_time,
    heads_time,
    scaled,
    grad_inner,
    grad_heads,
    out_heads,
    packed_grads,
    inner_tall,
    tall,
    low,
    high,
    bias,
    grads_time,
    grads_space,
    final_time,
    final_space,
    out_time,
    out_space,
    acc_time,
    acc_space,
    *scratch,
):
    at = Place()
    loads = [
        pltpu.make_async_copy(far, near, load_sems.at[i])
        for i, (far, near) in enumerate(
            (
                (cot_far, cot),
                (tokens_far, tokens),
                (w_spatial_qkv_far, w_spatial_qkv),
                (w_spatial_out_far, w_spatial_out),
                (w_temporal_out_far, w_temporal_out),
                (w_temporal_qkv_far, w_temporal_qkv),
            )
        )
    ]
    for load in loads:
        load.start()
    hail(at.friends())

    taken = 0

    def take(count):
        nonlocal taken
        taken += count
        return scratch[taken - count : taken]

    def trips(source, into, odd, odd_into):
        pairs = [(source.at[g], into.at[g]) for g in range(2)] + [(odd, odd_into)]
        return [Exchange(at, left, right, *take(3)) for left, right in pairs]

    cot_trips = trips(cot_blocks, cot_place, cot_odd, cot_odd_place)
    resid_trips = trips(resid_blocks, resid_place, resid_odd, resid_odd_place)
    grad_trips = trips(cot_blocks, grad_place, cot_odd, grad_odd_place)
    one = Reduction(at, grads_time, [acc_time, *take(3)], take(8))
    two = Reduction(at, grads_space, [acc_space, *take(3)], take(8))
    one_z = Depth(at, final_time, out_time, *take(1), take(6))
    two_z = Depth(at, final_space, out_space, *take(1), take(6))

    pad[...] = jnp.zeros_like(pad)
    loads[0].wait()
    for g in range(2):
        cot_blocks[g] = as_blocks(wide(cot[g * GROUP : (g + 1) * GROUP, :]))
    flat[2 * GROUP : ROWS, :] = wide(cot[2 * GROUP : ROWS, :])
    fold_odd(flat, 2 * GROUP, ODD, pad, cot_odd)
    meet(at.friends())
    for trip in cot_trips:
        trip.start()

    every = slice(0, ROWS)
    normed = cot
    loads[1].wait()
    normed[...] = modulated(wide(tokens[...]), mod, 0)
    loads[2].wait()
    project_rows(normed, every, w_spatial_qkv, packed, every)
    spread_heads(packed, heads, 3 * HEADS, every)
    loads[3].wait()

    def residual(first, last):
        rows = slice(first, last)
        attend_spatial(heads, mixed_heads, rows)
        for h in range(HEADS):
            mixed[rows, h * HEAD_DIM : (h + 1) * HEAD_DIM] = mixed_heads[h, rows]
        for start, width in columns(D):
            cols = slice(start, start + width)
            product = matmul(mixed[rows, :], w_spatial_out[:, cols])
            flat[rows, cols] = wide(tokens[rows, cols]) + mod[2][:, cols] * product

    residual(GROUP, ROWS)
    resid_blocks[1] = as_blocks(flat[GROUP : 2 * GROUP, :])
    resid_trips[1].start()
    fold_odd(flat, 2 * GROUP, ODD, pad, resid_odd)
    resid_trips[2].start()
    residual(0, GROUP)
    resid_blocks[0] = as_blocks(flat[0:GROUP, :])
    resid_trips[0].start()

    limit = lengths[0].astype(jnp.float32)

    def frame_of(index):
        return jnp.floor(index * (1.0 / SPAN))

    keys = lax.broadcasted_iota(jnp.int32, (GROUP, 1), 0).astype(jnp.float32)
    queries = lax.broadcasted_iota(jnp.int32, (1, GROUP), 1).astype(jnp.float32)
    same = (keys - SPAN * frame_of(keys)) == (queries - SPAN * frame_of(queries))
    bias[...] = jnp.where(same & (frame_of(keys) < limit), 0.0, MASKED)

    def frames(place, g):
        return wide(place[g]).reshape(GROUP, D)

    def masked_rows(g):
        return jnp.where(frame_of(keys) < limit, 1.0, 0.0) * frames(cot_place, g)

    def settle_odd(trip, odd_place, place):
        trip.arrive()
        flat[0:GROUP, :] = jnp.zeros((GROUP, D), jnp.float32)
        unfold_odd(odd_place, pad, flat, 0, SPAN)
        place[2] = as_blocks(flat[0:GROUP, :])

    for g in range(2):
        cot_trips[g].arrive()
    settle_odd(cot_trips[2], cot_odd_place, cot_place)
    for g in range(GROUPS):
        scaled[g * GROUP : (g + 1) * GROUP, :] = (mod[5] * masked_rows(g)).astype(HALF16)
    loads[4].wait()
    grad_inner[...] = matmul(scaled[...], w_temporal_out[...], NT).astype(HALF16)
    spread_heads(grad_inner, grad_heads, HEADS, slice(0, SPREAD))
    for trip in cot_trips:
        trip.settle()
    loads[5].wait()

    def temporal(members):
        count = len(members) * GROUP
        here, rows = slice(0, count), slice(members[0] * GROUP, members[0] * GROUP + count)
        for g in members:
            if g == 2:
                settle_odd(resid_trips[g], resid_odd_place, resid_place)
            else:
                resid_trips[g].arrive()
            normed_time[g * GROUP : (g + 1) * GROUP, :] = modulated(frames(resid_place, g), mod, 3)
        project_rows(normed_time, rows, w_temporal_qkv, packed_time, here)
        spread_heads(packed_time, heads_time, 3 * HEADS, here)

        def body(h, _):
            inner = pl.ds(pl.multiple_of(h * HEAD_DIM, 8), HEAD_DIM)
            for i, g in enumerate(members):
                part, whole_rows = slice(i * GROUP, (i + 1) * GROUP), slice(g * GROUP, (g + 1) * GROUP)
                values = heads_time[2 * HEADS + h, part]
                grad_queries, grad_keys, grad_values, soft = head_back(
                    heads_time[h, part],
                    heads_time[HEADS + h, part],
                    values,
                    grad_heads[h, whole_rows],
                    bias[...],
                )
                inner_tall[inner, whole_rows] = matmul(values, soft, TN)
                out_heads[h, part] = grad_queries
                out_heads[HEADS + h, part] = grad_keys
                out_heads[2 * HEADS + h, part] = grad_values
            return 0

        lax.fori_loop(0, HEADS, body, 0, unroll=UNROLL)
        for i in range(3 * HEADS):
            packed_grads[rows, i * HEAD_DIM : (i + 1) * HEAD_DIM] = out_heads[i, here]
        upstream_of(packed_grads, rows, w_temporal_qkv, low, count)
        for i, g in enumerate(members):
            total = masked_rows(g) + norm_pullback(
                frames(resid_place, g), upstream_rows(low, i * GROUP, GROUP), 1.0 + mod[4]
            )
            if g == 2:
                flat[0:GROUP, :] = total
                fold_odd(flat, 0, SPAN, pad, cot_odd)
            else:
                cot_blocks[g] = as_blocks(total)
            grad_trips[g].start()

    temporal((1, 2))
    temporal((0,))
    transposed(normed_time, SPREAD, tall)
    qkv_blocks(SPREAD, tall, packed_grads, grads_time)
    out_blocks(SPREAD, inner_tall, scaled, low, high, grads_time)
    one.start()

    transposed(normed, ROWS, tall)
    inner_tall[:, every] = wide(mixed[...]).T
    for g in (1, 2, 0):
        grad_trips[g].arrive()
    unfold_odd(grad_odd_place, pad, flat, 2 * GROUP, ODD)
    for g in range(2):
        flat[g * GROUP : (g + 1) * GROUP, :] = frames(grad_place, g)
    scaled[every, :] = (mod[2] * flat[...]).astype(HALF16)
    grad_inner[every, :] = matmul(scaled[every, :], w_spatial_out[...], NT).astype(HALF16)
    spread_heads(grad_inner, grad_heads, HEADS, every)
    one.first()
    one.second()
    out_blocks(ROWS, inner_tall, scaled, low, high, grads_space)

    def attend_back(h, _):
        grad_queries, grad_keys, grad_values, _ = head_back(
            heads[h], heads[HEADS + h], heads[2 * HEADS + h], grad_heads[h, every]
        )
        out_heads[h] = grad_queries
        out_heads[HEADS + h] = grad_keys
        out_heads[2 * HEADS + h] = grad_values
        return 0

    lax.fori_loop(0, HEADS, attend_back, 0, unroll=UNROLL)
    one.third()
    for i in range(3 * HEADS):
        packed_grads[every, i * HEAD_DIM : (i + 1) * HEAD_DIM] = out_heads[i]
    qkv_blocks(ROWS, tall, packed_grads, grads_space)
    two.start()
    upstream_of(packed_grads, every, w_spatial_qkv, low, ROWS)
    one.fourth()
    two.first()
    two.second()
    grad_tokens[...] = (
        flat[...]
        + norm_pullback(wide(tokens[...]), upstream_rows(low, 0, ROWS), 1.0 + mod[1])
    ).astype(HALF16)
    one.fifth(final_time)
    one_z.start()
    two.third()
    one_z.middle()
    two.fourth()
    one_z.end()
    two.fifth(final_space)
    two_z.start()
    assemble(out_time, summed, 0)
    two_z.middle()
    two_z.end()
    assemble(out_space, summed, WIDE)
    for user in resid_trips + grad_trips + [one, two, one_z, two_z]:
        user.settle()


def vmem(shape, dtype=HALF16):
    return pltpu.VMEM(shape, dtype)


def run(lengths, mod, tokens, cotangent, w_spatial_qkv, w_spatial_out, w_temporal_qkv, w_temporal_out):
    full = jnp.float32
    sent, place, odd = vmem((2, BLOCKS, SPAN, D)), vmem((GROUPS, BLOCKS, SPAN, D)), vmem((BLOCKS, SPAN, NARROW))
    scratch = [
        vmem((ROWS, D)),
        vmem((ROWS, D)),
        vmem((QKV, D)),
        vmem((INNER, D)),
        vmem((QKV, D)),
        vmem((INNER, D)),
        pltpu.SemaphoreType.DMA((6,)),
        sent,
        place,
        sent,
        place,
        sent,
        odd,
        odd,
        odd,
        odd,
        odd,
        vmem((GROUP, NARROW), full),
        vmem((ROWS, D), full),
        vmem((ROWS, QKV)),
        vmem((3 * HEADS, ROWS, HEAD_DIM)),
        vmem((HEADS, ROWS, HEAD_DIM)),
        vmem((ROWS, INNER)),
        vmem((SPREAD, D)),
        vmem((2 * GROUP, QKV)),
        vmem((3 * HEADS, 2 * GROUP, HEAD_DIM)),
        vmem((SPREAD, D)),
        vmem((SPREAD, INNER)),
        vmem((HEADS, SPREAD, HEAD_DIM)),
        vmem((3 * HEADS, ROWS, HEAD_DIM)),
        vmem((SPREAD, QKV)),
        vmem((INNER, SPREAD), full),
        vmem((D, SPREAD)),
        vmem((D, SPREAD), full),
        vmem((D, SPREAD), full),
        vmem((GROUP, GROUP), full),
        vmem((BLOCKS, 72, WIDE)),
        vmem((BLOCKS, 72, WIDE)),
        vmem((9, 72, 128)),
        vmem((9, 72, 128)),
        vmem((2, 9, 72, 128)),
        vmem((2, 9, 72, 128)),
        vmem((BLOCKS, 72, HALF)),
        vmem((BLOCKS, 72, HALF)),
    ]
    for _ in range(3 * GROUPS):
        scratch += exchange_sems()
    for _ in range(2):
        scratch += reduction_buffers() + reduction_sems()
    for _ in range(2):
        scratch += [vmem((2, NZ, 72, 128))] + depth_sems()
    return pl.pallas_call(
        kernel,
        out_shape=(
            jax.ShapeDtypeStruct((ROWS, D), HALF16),
            jax.ShapeDtypeStruct((72, 2 * WIDE), HALF16),
        ),
        in_specs=[pl.BlockSpec(memory_space=pltpu.SMEM), pl.BlockSpec(memory_space=pltpu.VMEM)]
        + [pl.BlockSpec(memory_space=pl.ANY)] * 6,
        out_specs=(pl.BlockSpec(memory_space=pltpu.VMEM),) * 2,
        scratch_shapes=scratch,
        compiler_params=pltpu.CompilerParams(
            collective_id=0, has_side_effects=True, vmem_limit_bytes=VMEM_LIMIT
        ),
    )(lengths, mod, tokens, cotangent, w_spatial_qkv, w_spatial_out, w_temporal_qkv, w_temporal_out)


def unpack_grads(summed):
    tall = summed[:, QKV:]
    return summed[:, :QKV], jnp.concatenate([tall[:36], tall[36:]], axis=-1)


def local(
    tokens,
    cotangent,
    modulation,
    lengths,
    w_spatial_qkv,
    w_spatial_out,
    w_temporal_qkv,
    w_temporal_out,
):
    grad_tokens, summed = run(
        lengths,
        modulation.reshape(6, 1, D),
        tokens.reshape(ROWS, D),
        cotangent.reshape(ROWS, D),
        w_spatial_qkv.T,
        w_spatial_out,
        w_temporal_qkv.T,
        w_temporal_out,
    )
    temporal_qkv, temporal_out = unpack_grads(summed[:, :WIDE])
    spatial_qkv, spatial_out = unpack_grads(summed[:, WIDE:])
    return (
        grad_tokens.reshape(tokens.shape),
        spatial_qkv,
        spatial_out,
        temporal_qkv,
        temporal_out,
    )


def solution(mesh):
    placed = (
        P("dp", "seq", None, None),
        P("dp", "seq", None, None),
        P("dp", None, None),
        P("dp"),
        P(),
        P(),
        P(),
        P(),
    )
    return jax.shard_map(
        local,
        mesh=mesh,
        in_specs=placed,
        out_specs=(
            P("dp", "seq", None, None),
            P("seq", None),
            P("seq", None),
            P("seq", None),
            P("seq", None),
        ),
        check_vma=False,
    )
```

profile of v0, /device:TPU:1, one launch (start us, length us, event | category | flops | bytes accessed | tf_op | source)
XLA Modules:
  0.0 125.6 jit_solution(1820780302395411711)
XLA Ops:
  1.3 118.6 %shard_map.119 = (bf16[320,1152]{1,0:T(8,128)(2,1)}, bf16[72,4608]{1,0:T(8,128)(2,1)}) custom-call(s32[1]{0:T(128)S(6)} %copy.14.lengths, f32[6,1,1152]{2,1,0:T(1,128)} %bitcast.11, bf16[320,1152]{1,0:T(8,128)(2,1)} %bitcast.8, bf16[320,1152]{1,0:T(8,128)(2,1)} %bitcast.9, bf16[1728,1152]{1,0:T(8,128)(2,1)} %bitcast.6, bf16[576,1152]{1,0:T(8,128)(2,1)} %w_spatial_out_far.1, ...), custom_call_target="tpu_custom_call" | custom-call | tf_op jit(solution)/shard_map/pallas_call | solution.py:905
  119.9 1.0 fusion
  120.9 1.9 %fusion.1 = (bf16[72,1728]{1,0:T(8,128)(2,1)}, bf16[72,1728]{1,0:T(8,128)(2,1)}) fusion(bf16[72,4608]{1,0:T(8,128)(2,1)} %get-tuple-element.8), kind=kLoop, calls=%fused_computation.3 | loop fusion | bytes 995328 | tf_op jit(solution)/shard_map/slice | solution.py:923
  122.8 0.8 pad_maximum_fusion
  123.6 2.0 %copy.15 = bf16[1,1,320,1152]{3,2,1,0:T(8,128)(2,1)} copy(bf16[1,1,320,1152]{3,2,1,0:T(8,128)(2,1)} %bitcast.10) | data formatting | bytes 1474560
where the time goes:
time: 126 us
  Pallas kernels  119 us (94%)
  local copies, waits for them, and re-layouts  4.96 us (4%)
  between operations  1.3 us (1%)
    pallas_call x1, Pallas kernels, run(): pl.pallas_call(kernel, out_shape=(jax.ShapeDtypeStruct((ROWS, D), HALF16)...  119 us
    slice x2, local copies, waits for them, and re-layouts, unpack_grads(): return (summed[:, :QKV], jnp.concatenate([tall[:36], tall[36:]], axis=-1))  2.93 us

commit v1 on v0

--- a/solution.py
+++ b/solution.py
@@ -347,19 +347,32 @@
     def start(self):
         self.others(lambda i: self.up(i, self.place.z).start())
 
+    def add(self, i, tile, owner, slot):
+        at = self.place
+        spot = self.out.at[at.c, tile]
+        total = self.final[tile].astype(jnp.float32)
+        for d in range(1, NZ):
+            z = lax.rem(owner + d, NZ)
+            remote(
+                self.final.at[tile],
+                self.arrived.at[slot, z],
+                self.up_send.at[i],
+                self.up_recv.at[i, z],
+                self.device(owner),
+            ).wait_recv()
+            total = total + self.arrived[slot, z].astype(jnp.float32)
+        spot[...] = total.astype(jnp.bfloat16)
+        for d in range(1, NZ):
+            z = lax.rem(owner + d, NZ)
+            remote(
+                spot, spot, self.down_send.at[i, z], self.down_recv.at[i], self.device(z)
+            ).start()
+        remote(spot, spot, self.pair_send.at[i], self.pair_recv.at[i], at.twin).start()
+
     def middle(self):
-        def add(i):
-            tile, _, slot = TILES[i]
-            total = self.final[tile].astype(jnp.float32)
-            for z in self.away(i):
-                self.up(i, z).wait_recv()
-                total = total + self.arrived[slot, z].astype(jnp.float32)
-            self.spot(i, self.place.c)[...] = total.astype(jnp.bfloat16)
-            for z in self.away(i):
-                self.down(i, z).start()
-            self.pair(i, self.place.c).start()
-
-        self.owned(add)
+        z = self.place.z
+        self.add(z, z, z, 0)
+        pl.when(z == 0)(lambda: self.add(NZ, NZ, 0, 1))
 
     def end(self):
         def forward(i):
@@ -445,7 +458,11 @@
     return ref_value.astype(jnp.float32)
 
 
-def by_columns(total, width, body):
+def by_columns(total, width, body, looped):
+    if not looped:
+        for start, part in columns(total, width):
+            body(start, part)
+        return
     even = total // width * width
 
     @pl.loop(0, even, step=width)
@@ -461,7 +478,7 @@
         cols = pl.ds(start, width)
         out_ref[out_rows, cols] = matmul(rows_ref[rows, :], weight_ref[cols, :], NT).astype(HALF16)
 
-    by_columns(weight_ref.shape[0], 512, body)
+    by_columns(weight_ref.shape[0], 256, body, False)
 
 
 def spread_heads(wide_ref, heads_ref, count, rows):
@@ -499,7 +516,7 @@
     return grad_queries, grad_keys, grad_values, soft_rounded
 
 
-def qkv_blocks(depth, tall, packed_grads, grads):
+def qkv_blocks(depth, tall, packed_grads, grads, looped):
     deep = slice(0, depth)
 
     def body(start, width):
@@ -507,7 +524,7 @@
         product = matmul(tall[:, deep], packed_grads[deep, cols])
         grads[:, :, cols] = product.reshape(BLOCKS, 72, width).astype(HALF16)
 
-    by_columns(QKV, 256, body)
+    by_columns(QKV, 256, body, looped)
 
 
 def out_blocks(depth, inner_tall, cot, low, high, grads):
@@ -534,11 +551,11 @@
         tall_ref[cols, 0:count] = rows_ref[0:count, cols].T
 
 
-def upstream_of(packed_grads, rows, w_qkv, into, count):
+def upstream_of(packed_grads, rows, w_qkv, into, count, looped):
     def body(start, width):
         into[pl.ds(start, count), :] = matmul(packed_grads[rows, :], w_qkv[:, pl.ds(start, width)])
 
-    by_columns(D, SPREAD, body)
+    by_columns(D, SPREAD, body, looped)
 
 
 def upstream_rows(into, start, count):
@@ -564,8 +581,9 @@
 
 
 def assemble(tiles, summed, start):
-    for k in range(18):
-        summed[:, start + k * 128 : start + (k + 1) * 128] = tiles[k // 9, k % 9]
+    for core in range(2):
+        for k in range(9):
+            summed[core, :, start + k * 128 : start + (k + 1) * 128] = tiles[core, k]
 
 
 def as_blocks(rows):
@@ -679,7 +697,12 @@
     every = slice(0, ROWS)
     normed = cot
     loads[1].wait()
-    normed[...] = modulated(wide(tokens[...]), mod, 0)
+
+    def norm_rows(start):
+        rows = pl.ds(pl.multiple_of(start, ROWS // 2), ROWS // 2)
+        normed[rows, :] = modulated(wide(tokens[rows, :]), mod, 0)
+
+    pl.loop(0, ROWS, step=ROWS // 2)(norm_rows)
     loads[2].wait()
     project_rows(normed, every, w_spatial_qkv, packed, every)
     spread_heads(packed, heads, 3 * HEADS, every)
@@ -771,7 +794,7 @@
         lax.fori_loop(0, HEADS, body, 0, unroll=UNROLL)
         for i in range(3 * HEADS):
             packed_grads[rows, i * HEAD_DIM : (i + 1) * HEAD_DIM] = out_heads[i, here]
-        upstream_of(packed_grads, rows, w_temporal_qkv, low, count)
+        upstream_of(packed_grads, rows, w_temporal_qkv, low, count, False)
         for i, g in enumerate(members):
             total = masked_rows(g) + norm_pullback(
                 frames(resid_place, g), upstream_rows(low, i * GROUP, GROUP), 1.0 + mod[4]
@@ -786,7 +809,7 @@
     temporal((1, 2))
     temporal((0,))
     transposed(normed_time, SPREAD, tall)
-    qkv_blocks(SPREAD, tall, packed_grads, grads_time)
+    qkv_blocks(SPREAD, tall, packed_grads, grads_time, True)
     out_blocks(SPREAD, inner_tall, scaled, low, high, grads_time)
     one.start()
 
@@ -817,16 +840,24 @@
     one.third()
     for i in range(3 * HEADS):
         packed_grads[every, i * HEAD_DIM : (i + 1) * HEAD_DIM] = out_heads[i]
-    qkv_blocks(ROWS, tall, packed_grads, grads_space)
+    qkv_blocks(ROWS, tall, packed_grads, grads_space, False)
     two.start()
-    upstream_of(packed_grads, every, w_spatial_qkv, low, ROWS)
+    upstream_of(packed_grads, every, w_spatial_qkv, low, ROWS, True)
     one.fourth()
     two.first()
     two.second()
-    grad_tokens[...] = (
-        flat[...]
-        + norm_pullback(wide(tokens[...]), upstream_rows(low, 0, ROWS), 1.0 + mod[1])
-    ).astype(HALF16)
+
+    def last_rows(start):
+        count = ROWS // 2
+        rows = pl.ds(pl.multiple_of(start, count), count)
+        grad = jnp.concatenate(
+            [low[pl.ds(pl.multiple_of(n * SPREAD + start, 32), count), :] for n in range(3)], axis=-1
+        )
+        grad_tokens[rows, :] = (
+            flat[rows, :] + norm_pullback(wide(tokens[rows, :]), grad, 1.0 + mod[1])
+        ).astype(HALF16)
+
+    pl.loop(0, ROWS, step=ROWS // 2)(last_rows)
     one.fifth(final_time)
     one_z.start()
     two.third()
@@ -838,7 +869,7 @@
     assemble(out_time, summed, 0)
     two_z.middle()
     two_z.end()
-    assemble(out_space, summed, WIDE)
+    assemble(out_space, summed, HALF)
     for user in resid_trips + grad_trips + [one, two, one_z, two_z]:
         user.settle()
 
@@ -906,7 +937,7 @@
         kernel,
         out_shape=(
             jax.ShapeDtypeStruct((ROWS, D), HALF16),
-            jax.ShapeDtypeStruct((72, 2 * WIDE), HALF16),
+            jax.ShapeDtypeStruct((2, 72, WIDE), HALF16),
         ),
         in_specs=[pl.BlockSpec(memory_space=pltpu.SMEM), pl.BlockSpec(memory_space=pltpu.VMEM)]
         + [pl.BlockSpec(memory_space=pl.ANY)] * 6,
@@ -918,9 +949,13 @@
     )(lengths, mod, tokens, cotangent, w_spatial_qkv, w_spatial_out, w_temporal_qkv, w_temporal_out)
 
 
-def unpack_grads(summed):
-    tall = summed[:, QKV:]
-    return summed[:, :QKV], jnp.concatenate([tall[:36], tall[36:]], axis=-1)
+def unpack_grads(summed, item):
+    left, right = (half[:, item * HALF : (item + 1) * HALF] for half in (summed[0], summed[1]))
+    tall = right[:, QKV - HALF :]
+    return (
+        jnp.concatenate([left, right[:, : QKV - HALF]], axis=-1),
+        jnp.concatenate([tall[:36], tall[36:]], axis=-1),
+    )
 
 
 def local(
@@ -943,8 +978,8 @@
         w_temporal_qkv.T,
         w_temporal_out,
     )
-    temporal_qkv, temporal_out = unpack_grads(summed[:, :WIDE])
-    spatial_qkv, spatial_out = unpack_grads(summed[:, WIDE:])
+    temporal_qkv, temporal_out = unpack_grads(summed, 0)
+    spatial_qkv, spatial_out = unpack_grads(summed, 1)
     return (
         grad_tokens.reshape(tokens.shape),
         spatial_qkv,

time: 126 us -> 120 us (0.952)
  Pallas kernels: 119 us -> 115 us
  local copies, waits for them, and re-layouts: 4.96 us -> 2.23 us
    pallas_call x1, Pallas kernels: 119 us -> 115 us  [run(): pl.pallas_call(kernel, out_shape=(jax.ShapeDtypeStruct((ROWS, D), HALF16)...]
    slice x2 -> x3, local copies, waits for them, and re-layouts: 2.93 us -> 0.17 us  [the longest x1 0.13 us: unpack_grads(): tall[:36]]
where the time goes in v1:
time: 120 us
  Pallas kernels  115 us (96%)
  local copies, waits for them, and re-layouts  2.23 us (2%)
  other arithmetic  1.59 us (1%)
  between operations  1.32 us (1%)
    pallas_call x1, Pallas kernels, run(): pl.pallas_call(kernel, out_shape=(jax.ShapeDtypeStruct((ROWS, D), HALF16)...  115 us

profile of v1, /device:TPU:1, one launch (start us, length us, event | category | flops | bytes accessed | tf_op | source)
XLA Modules:
  0.0 120.2 jit_solution(4075618057926655985)
XLA Ops:
  1.3 115.1 %shard_map.119 = (bf16[320,1152]{1,0:T(8,128)(2,1)}, bf16[2,72,2304]{2,1,0:T(8,128)(2,1)}) custom-call(s32[1]{0:T(128)S(6)} %copy.14.lengths, f32[6,1,1152]{2,1,0:T(1,128)} %bitcast.15, bf16[320,1152]{1,0:T(8,128)(2,1)} %bitcast.12, bf16[320,1152]{1,0:T(8,128)(2,1)} %bitcast.13, bf16[1728,1152]{1,0:T(8,128)(2,1)} %bitcast.10, ...), custom_call_target="tpu_custom_call" | custom-call | tf_op jit(solution)/shard_map/pallas_call | solution.py:936
  116.4 0.0 copy-start
  116.4 1.2 slice_bitcast_fusion.1
  117.6 0.1 fusion
  117.8 0.8 pad_maximum_fusion.2
  118.5 0.8 pad_maximum_fusion
  119.4 0.0 copy-done
  119.4 0.9 copy.15
  (2 shorter events, 0.0 us)
Async XLA Ops:
  116.4 3.0 %copy-start = (bf16[320,1152]{1,0:T(8,128)(2,1)S(1)}, bf16[320,1152]{1,0:T(8,128)(2,1)}, u32[]{:S(2)}) copy-start(bf16[320,1152]{1,0:T(8,128)(2,1)} %get-tuple-element.7) | copy-start | bytes 2211844

commit v2 on v1

--- a/solution.py
+++ b/solution.py
@@ -843,9 +843,9 @@
     qkv_blocks(ROWS, tall, packed_grads, grads_space, False)
     two.start()
     upstream_of(packed_grads, every, w_spatial_qkv, low, ROWS, True)
-    one.fourth()
     two.first()
     two.second()
+    one.fourth()
 
     def last_rows(start):
         count = ROWS // 2

time: 120 us -> 126 us (1.050)
  Pallas kernels: 115 us -> 120 us
    pallas_call x1, Pallas kernels: 115 us -> 120 us  [run(): pl.pallas_call(kernel, out_shape=(jax.ShapeDtypeStruct((ROWS, D), HALF16)...]
where the time goes in v2:
time: 126 us
  Pallas kernels  120 us (95%)
  local copies, waits for them, and re-layouts  2.23 us (2%)
  other arithmetic  1.59 us (1%)
  between operations  1.32 us (1%)
    pallas_call x1, Pallas kernels, run(): pl.pallas_call(kernel, out_shape=(jax.ShapeDtypeStruct((ROWS, D), HALF16)...  120 us

profile of v2, /device:TPU:1, one launch (start us, length us, event | category | flops | bytes accessed | tf_op | source)
XLA Modules:
  0.0 125.5 jit_solution(3780838983047335046)
XLA Ops:
  1.3 120.4 %shard_map.119 = (bf16[320,1152]{1,0:T(8,128)(2,1)}, bf16[2,72,2304]{2,1,0:T(8,128)(2,1)}) custom-call(s32[1]{0:T(128)S(6)} %copy.14.lengths, f32[6,1,1152]{2,1,0:T(1,128)} %bitcast.15, bf16[320,1152]{1,0:T(8,128)(2,1)} %bitcast.12, bf16[320,1152]{1,0:T(8,128)(2,1)} %bitcast.13, bf16[1728,1152]{1,0:T(8,128)(2,1)} %bitcast.10, ...), custom_call_target="tpu_custom_call" | custom-call | tf_op jit(solution)/shard_map/pallas_call | solution.py:936
  121.7 0.0 copy-start
  121.7 1.2 slice_bitcast_fusion.1
  122.9 0.1 fusion
  123.1 0.8 pad_maximum_fusion.2
  123.8 0.8 pad_maximum_fusion
  124.7 0.0 copy-done
  124.7 0.9 copy.15
  (2 shorter events, 0.0 us)
Async XLA Ops:
  121.7 3.0 %copy-start = (bf16[320,1152]{1,0:T(8,128)(2,1)S(1)}, bf16[320,1152]{1,0:T(8,128)(2,1)}, u32[]{:S(2)}) copy-start(bf16[320,1152]{1,0:T(8,128)(2,1)} %get-tuple-element.7) | copy-start | bytes 2211844

commit v3 on v2

--- a/solution.py
+++ b/solution.py
@@ -842,10 +842,10 @@
         packed_grads[every, i * HEAD_DIM : (i + 1) * HEAD_DIM] = out_heads[i]
     qkv_blocks(ROWS, tall, packed_grads, grads_space, False)
     two.start()
+    one.fourth()
     upstream_of(packed_grads, every, w_spatial_qkv, low, ROWS, True)
     two.first()
     two.second()
-    one.fourth()
 
     def last_rows(start):
         count = ROWS // 2

time: 126 us -> 120 us (0.952)
  Pallas kernels: 120 us -> 115 us
    pallas_call x1, Pallas kernels: 120 us -> 115 us  [run(): pl.pallas_call(kernel, out_shape=(jax.ShapeDtypeStruct((ROWS, D), HALF16)...]
where the time goes in v3:
time: 120 us
  Pallas kernels  115 us (96%)
  local copies, waits for them, and re-layouts  2.23 us (2%)
  other arithmetic  1.59 us (1%)
  between operations  1.32 us (1%)
    pallas_call x1, Pallas kernels, run(): pl.pallas_call(kernel, out_shape=(jax.ShapeDtypeStruct((ROWS, D), HALF16)...  115 us

profile of v3, /device:TPU:1, one launch (start us, length us, event | category | flops | bytes accessed | tf_op | source)
XLA Modules:
  0.0 120.3 jit_solution(17843745844721106865)
XLA Ops:
  1.3 115.1 %shard_map.119 = (bf16[320,1152]{1,0:T(8,128)(2,1)}, bf16[2,72,2304]{2,1,0:T(8,128)(2,1)}) custom-call(s32[1]{0:T(128)S(6)} %copy.14.lengths, f32[6,1,1152]{2,1,0:T(1,128)} %bitcast.15, bf16[320,1152]{1,0:T(8,128)(2,1)} %bitcast.12, bf16[320,1152]{1,0:T(8,128)(2,1)} %bitcast.13, bf16[1728,1152]{1,0:T(8,128)(2,1)} %bitcast.10, ...), custom_call_target="tpu_custom_call" | custom-call | tf_op jit(solution)/shard_map/pallas_call | solution.py:936
  116.4 0.0 copy-start
  116.4 1.2 slice_bitcast_fusion.1
  117.7 0.1 fusion
  117.8 0.8 pad_maximum_fusion.2
  118.6 0.8 pad_maximum_fusion
  119.4 0.0 copy-done
  119.4 0.9 copy.15
  (2 shorter events, 0.0 us)
Async XLA Ops:
  116.4 3.0 %copy-start = (bf16[320,1152]{1,0:T(8,128)(2,1)S(1)}, bf16[320,1152]{1,0:T(8,128)(2,1)}, u32[]{:S(2)}) copy-start(bf16[320,1152]{1,0:T(8,128)(2,1)} %get-tuple-element.7) | copy-start | bytes 2211844
